TPU v7x, 32 devices: a whole 2x2x4 slice. The times are simulated.
32 devices in a mesh: gx: 4 (over z), yz: 8 (over y, x, core).
Axes of the slice: x: 2, y: 2, z: 4, core: 2. Of those that a mesh axis runs over, the one named last changes fastest.
Arguments:
- states_in: bfloat16 [256, 18432], P(None, 'gx'), may hold values from -80 to 80
- norm_gain: float32 [18432], P('gx'), may hold values from 0.1 to 1.9
- w_query: bfloat16 [18432, 12288], P('gx', 'yz'), may hold values from -0.046875 to 0.046875
- w_keyval: bfloat16 [18432, 512], P('gx', 'yz'), may hold values from -0.046875 to 0.046875
- w_out: bfloat16 [12288, 18432], P('yz', 'gx'), may hold values from -0.4375 to 0.4375
- key_cache: bfloat16 [256, 2048, 256], P(('gx', 'yz')), may hold values from -128 to 128
- value_cache: bfloat16 [256, 2048, 256], P(('gx', 'yz')), may hold values from -6 to 6
- lengths: int32 [256], P(('gx', 'yz')), may hold values from 1 to 2048, as said below
- positions: int32 [256], replicated, may hold values from 1 to 4095, as said below
Outputs:
- states: bfloat16 [2, 256, 18432], P(None, 'yz', 'gx')
- new_kv: bfloat16 [2, 256, 512], P(None, ('gx', 'yz'))
Inputs may be any that keep to these rules, and one draw needn't show every extreme that they name: `lengths`: at least one row has exactly 2048 valid slots. positions[b] >= lengths[b]; the token of step t stands at positions[b] + t.
All inputs are finite; a program needn't handle non-finite values.
Results may differ from a plain program's by a relative error of at most 0.025.
Values may be sent and summed in bfloat16 or wider, within the bound.
A program may use at most 128 MiB of HBM per device.

v0:
```python
import math

import jax
import jax.numpy as jnp
from jax import lax
from jax.sharding import PartitionSpec as P

D = 18432
DH = 256
STEPS = 2


epsilon = 1e-06
floor_score = -1e30


def rotary(vectors, places):
    half_width = vectors.shape[-1] // 2
    frequency = jnp.exp(
        jnp.arange(half_width, dtype=jnp.float32) * (-2.0 * math.log(10000.0) / vectors.shape[-1])
    )
    angles = places.astype(jnp.float32)[..., None] * frequency
    cosine = jnp.cos(angles)
    sine_part = jnp.sin(angles)
    leading = vectors[..., :half_width]
    trailing = vectors[..., half_width:]
    return jnp.concatenate(
        [leading * cosine - trailing * sine_part, trailing * cosine + leading * sine_part], axis=-1
    )


def layer_norm(hidden, norm_gain):
    values = hidden.astype(jnp.float32)
    totals = lax.psum(jnp.sum(values, axis=1), "gx")
    center = totals / D
    offset = values - center[:, None]
    spread = lax.psum(jnp.sum(offset * offset, axis=1), "gx") / D
    return ((values - center[:, None]) * lax.rsqrt(spread + epsilon)[:, None] * norm_gain).astype(
        jnp.bfloat16
    )


def attend(queries, key_cache, value_cache, lengths, extra_keys, extra_values):
    score_scale = 1.0 / math.sqrt(queries.shape[-1])
    extra_scores = (
        jnp.einsum("rhd,rtd->rht", queries, extra_keys, preferred_element_type=jnp.float32)
        * score_scale
    )
    scores = (
        jnp.einsum("rhd,rsd->rhs", queries, key_cache, preferred_element_type=jnp.float32)
        * score_scale
    )
    usable = jnp.arange(key_cache.shape[1])[None, :] < lengths[:, None]
    scores = jnp.where(usable[:, None, :], scores, floor_score)
    row_top = jnp.maximum(jnp.max(scores, axis=2), jnp.max(extra_scores, axis=2))[..., None]
    cached_weights = jnp.exp(scores - row_top)
    extra_weights = jnp.exp(extra_scores - row_top)
    weight_sum = jnp.sum(cached_weights, axis=2) + jnp.sum(extra_weights, axis=2)
    weighted = jnp.einsum(
        "rhs,rsd->rhd",
        cached_weights.astype(jnp.bfloat16),
        value_cache,
        preferred_element_type=jnp.float32,
    )
    weighted = weighted + jnp.einsum(
        "rht,rtd->rhd",
        extra_weights.astype(jnp.bfloat16),
        extra_values,
        preferred_element_type=jnp.float32,
    )
    return (weighted / weight_sum[..., None]).astype(jnp.bfloat16)


def on_device(
    states_in, norm_gain, w_query, w_keyval, w_out, key_cache, value_cache, lengths, positions
):
    gx_count = lax.axis_size("gx")
    yz_count = lax.axis_size("yz")
    gx_index = lax.axis_index("gx")
    yz_index = lax.axis_index("yz")
    row_dev = key_cache.shape[0]
    total_rows = states_in.shape[0]
    block_rows = total_rows // gx_count
    share_rows = total_rows // yz_count
    head_width = w_query.shape[1]
    own_start = (gx_index * yz_count + yz_index) * row_dev
    own_positions = lax.dynamic_slice_in_dim(positions, own_start, row_dev)
    block_positions = lax.dynamic_slice_in_dim(positions, gx_index * block_rows, block_rows)
    own_rows = lax.dynamic_slice_in_dim(states_in, yz_index * share_rows, share_rows, 0)
    normed = layer_norm(states_in, norm_gain)
    new_keys = []
    new_values = []
    results = []
    for step_index in range(STEPS):

        def project(start, count, normed=normed):
            return jnp.concatenate(
                [
                    jnp.dot(normed, w_query, preferred_element_type=jnp.float32),
                    jnp.dot(normed, w_keyval, preferred_element_type=jnp.float32),
                ],
                axis=1,
            )

        summed = lax.psum_scatter(
            project(jnp.int32(0), block_rows * lax.axis_size("gx")),
            "gx",
            scatter_dimension=0,
            tiled=True,
        )
        query_sum = summed[:, :head_width].reshape(block_rows, -1, DH)
        query_block = (
            rotary(query_sum, block_positions[:, None] + step_index)
            .reshape(block_rows, head_width)
            .astype(jnp.bfloat16)
        )
        keyval_block = summed[:, head_width:].astype(jnp.bfloat16)
        query_own, keyval_own = (
            lax.all_to_all(query_block, "yz", split_axis=0, concat_axis=1, tiled=True),
            lax.all_to_all(keyval_block, "yz", split_axis=0, concat_axis=1, tiled=True),
        )
        key_new = rotary(keyval_own[:, :DH].astype(jnp.float32), own_positions + step_index).astype(
            jnp.bfloat16
        )
        new_keys.append(key_new)
        new_values.append(keyval_own[:, DH:])
        attended = attend(
            query_own.reshape(row_dev, -1, DH),
            key_cache,
            value_cache,
            lengths,
            jnp.stack(new_keys, axis=1),
            jnp.stack(new_values, axis=1),
        )
        heads_block = lax.all_to_all(
            attended.reshape(row_dev, -1), "yz", split_axis=1, concat_axis=0, tiled=True
        )
        partial_out = jnp.dot(
            lax.all_gather(heads_block, "gx", axis=0, tiled=True),
            w_out,
            preferred_element_type=jnp.float32,
        )
        own_sum = lax.psum_scatter(partial_out, "yz", scatter_dimension=0, tiled=True)
        own_rows = (own_rows.astype(jnp.float32) + own_sum).astype(jnp.bfloat16)
        results.append(own_rows)
        if step_index + 1 < STEPS:
            normed = lax.all_gather(layer_norm(own_rows, norm_gain), "yz", axis=0, tiled=True)
    new_kv = jnp.stack(
        [
            jnp.concatenate([key_part, value_part], axis=1)
            for key_part, value_part in zip(new_keys, new_values)
        ]
    )
    return (jnp.stack(results), new_kv)


def solution(mesh):
    in_specs = (
        P(None, "gx"),
        P("gx"),
        P("gx", "yz"),
        P("gx", "yz"),
        P("yz", "gx"),
        P(("gx", "yz"), None, None),
        P(("gx", "yz"), None, None),
        P(("gx", "yz")),
        P(),
    )
    out_specs = (P(None, "yz", "gx"), P(None, ("gx", "yz"), None))
    return jax.shard_map(
        on_device, mesh=mesh, in_specs=in_specs, out_specs=out_specs, check_vma=False
    )
```

profile of v0, /device:TPU:0, one launch (start us, length us, event | category | flops | bytes accessed | tf_op | source)
XLA Modules:
  0.0 426.0 jit_solution(16196232650789743277)
XLA Ops:
  7.2 2.2 convert_reduce_fusion
  9.5 13.5 %psum.28 = f32[256]{0:T(256)S(1)} all-reduce(f32[256]{0:T(256)S(1)} %convert_reduce_fusion), channel_id=1, replica_groups=mesh['gx'=4,'yz'=8] {'gx'}, use_global_device_ids=true, to_apply=%region_1.0 | all-reduce | flops 256 | bytes 2048 | tf_op jit(solution)/shard_map/psum | solution.py:34
  22.9 0.8 fusion.2
  23.7 8.4 %psum.29 = f32[256]{0:T(256)S(1)} all-reduce(f32[256]{0:T(256)S(1)} %fusion.2), channel_id=1, replica_groups=mesh['gx'=4,'yz'=8] {'gx'}, use_global_device_ids=true, to_apply=%region_3.0 | all-reduce | flops 256 | bytes 2048 | tf_op jit(solution)/shard_map/psum | solution.py:37
  32.1 0.9 fusion.78
  33.0 7.3 %fusion.80 = f32[256,1536]{1,0:T(8,128)S(1)} fusion(bf16[4608,1536]{1,0:T(8,128)(2,1)} %param.11, bf16[256,4608]{1,0:T(8,128)(2,1)S(1)} %copy-done.2, f32[4608]{0:T(1024)S(1)} %copy-done.3, f32[256]{0:T(256)S(1)} %add_rsqrt_fusion, f32[256]{0:T(256)S(1)} %broadcast_multiply_fusion), kind=kOutput, calls=%fused_computation.117 | convolution fusion | flops 3629776896 | bytes 18108416 | tf_op jit(solution)/shard_map/dot_general | solution.py:99
  40.3 1.3 pad_maximum_fusion
  41.7 0.6 add_convert_fusion.3
  42.3 0.8 multiply_cosine_fusion
  43.2 35.5 %reduce-scatter.5.cloned.1.call-done = f32[64,1600]{1,0:T(8,128)} async-done(((f32[256,1600]{1,0:T(8,128)}), f32[64,1600]{1,0:T(8,128)}) %reduce-scatter.5.cloned.1.call-update) | async-done | bytes 409616 | tf_op jit(solution)/shard_map/reduce_scatter | solution.py:105
  78.7 0.8 fusion.40
  79.5 0.7 reshape.292
  80.2 4.0 all-to-all-start.1
  84.2 1.8 slice.66
  85.9 1.1 reshape.286
  87.0 0.8 subtract_convert_fusion.1
  88.0 0.9 convert_element_type.94
  88.9 4.1 all-to-all-start
  93.0 0.8 reshape.293
  93.9 0.7 fusion.71
  94.7 4.5 %all-to-all-done = bf16[8,8,1536]{2,1,0:T(8,128)(2,1)S(1)} async-done(((bf16[8,8,1536]{2,1,0:T(8,128)(2,1)}), bf16[8,8,1536]{2,1,0:T(8,128)(2,1)S(1)}, u32[]{:S(2)}, u32[]{:S(2)}) %all-to-all-start) | async-done | bytes 196640 | tf_op jit(solution)/shard_map/all_to_all | solution.py:119
  99.3 0.2 reshape.287
  99.5 0.1 fusion.53
  99.6 6.3 %fusion.84 = (f32[8,48]{1,0:T(8,128)S(1)}, f32[8,48,2048]{2,1,0:T(8,128)S(1)}) fusion(bf16[8,48,256]{2,1,0:T(8,128)(2,1)S(1)} %reshape.287, bf16[8,2048,256]{2,1,0:T(8,128)(2,1)} %param.14, pred[8,2048]{1,0:T(8,128)(4,1)S(1)} %iota_compare_fusion), kind=kOutput, calls=%fused_computation.120 | convolution fusion | flops 405012096 | bytes 11748864 | tf_op jit(solution)/shard_map/rhd,rsd->rhs/dot_general | solution.py:50
  105.9 0.6 fusion.5
  106.5 1.6 fusion.27
  108.1 0.2 all_to_all.82
  108.4 8.6 %all_to_all.102 = bf16[8,8,1536]{2,0,1:T(8,128)(2,1)S(1)} all-to-all(bf16[8,8,1536]{2,0,1:T(8,128)(2,1)S(1)} %copy.84), channel_id=1, replica_groups=mesh['gx'=4,'yz'=8] {'yz'}, dimensions={1} | all-to-all | bytes 393216 | tf_op jit(solution)/shard_map/all_to_all | solution.py:135
  117.0 18.2 %all_gather.9 = bf16[256,1536]{1,0:T(8,128)(2,1)S(1)} all-gather(bf16[64,1536]{1,0:T(8,128)(2,1)S(1)} %bitcast.56), channel_id=1, replica_groups=mesh['gx'=4,'yz'=8] {'gx'}, dimensions={0}, use_global_device_ids=true | all-gather | bytes 983040 | tf_op jit(solution)/shard_map/all_gather | solution.py:139
  135.2 10.5 %fusion.87 = f32[256,4608]{1,0:T(8,128)} fusion(bf16[256,1536]{1,0:T(8,128)(2,1)S(1)} %all_gather.9, bf16[1536,4608]{1,0:T(8,128)(2,1)} %param.13), kind=kOutput, calls=%fused_computation.123 | convolution fusion | flops 3623878656 | bytes 19660800 | tf_op jit(solution)/shard_map/dot_general | solution.py:138
  145.8 51.7 %reduce-scatter.7.cloned.1.call-done = f32[32,4608]{1,0:T(8,128)} async-done(((f32[256,4608]{1,0:T(8,128)}), f32[32,4608]{1,0:T(8,128)}) %reduce-scatter.7.cloned.1.call-update) | async-done | bytes 589840 | tf_op jit(solution)/shard_map/reduce_scatter | solution.py:143
  197.4 1.2 convert_reduce_fusion.1
  198.7 11.7 %psum.30 = f32[32]{0:T(128)S(1)} all-reduce(f32[32]{0:T(128)S(1)} %get-tuple-element.2), channel_id=1, replica_groups=mesh['gx'=4,'yz'=8] {'gx'}, use_global_device_ids=true, to_apply=%region_9.10 | all-reduce | flops 32 | bytes 256 | tf_op jit(solution)/shard_map/psum | solution.py:34
  210.4 0.3 fusion.35
  210.7 8.4 %psum.31 = f32[32]{0:T(128)S(1)} all-reduce(f32[32]{0:T(128)S(1)} %fusion.35), channel_id=1, replica_groups=mesh['gx'=4,'yz'=8] {'gx'}, use_global_device_ids=true, to_apply=%region_11.12 | all-reduce | flops 32 | bytes 256 | tf_op jit(solution)/shard_map/psum | solution.py:37
  219.0 0.9 fusion.37
  220.0 27.8 %all-gather.2.cloned.1.call-done = bf16[256,4608]{1,0:T(8,128)(2,1)} async-done(((bf16[32,4608]{1,0:T(8,128)(2,1)}), bf16[256,4608]{1,0:T(8,128)(2,1)}) %all-gather.2.cloned.1.call-update) | async-done | bytes 2359312 | tf_op jit(solution)/shard_map/all_gather | solution.py:147
  247.8 2.4 fusion.89
  250.2 7.7 %fusion.88 = f32[256,1536]{1,0:T(8,128)S(1)} fusion(bf16[256,4608]{1,0:T(8,128)(2,1)} %all-gather.2.cloned.1.call-done, bf16[4608,1536]{1,0:T(8,128)(2,1)} %param.11), kind=kOutput, calls=%fused_computation.124 | convolution fusion | flops 3623878656 | bytes 18087936 | tf_op jit(solution)/shard_map/dot_general | solution.py:99
  257.9 1.3 pad_maximum_fusion.1
  259.3 37.4 %reduce-scatter.9.cloned.1.call-done = f32[64,1600]{1,0:T(8,128)} async-done(((f32[256,1600]{1,0:T(8,128)}), f32[64,1600]{1,0:T(8,128)}) %reduce-scatter.9.cloned.1.call-update) | async-done | bytes 409616 | tf_op jit(solution)/shard_map/reduce_scatter | solution.py:105
  296.7 0.8 fusion.41
  297.5 0.7 reshape.294
  298.2 3.7 all-to-all-start.4
  301.8 1.0 slice.74
  303.1 0.9 convert_element_type.104
  304.0 2.5 all-to-all-done.4
  306.5 3.4 all-to-all-start.3
  310.2 0.1 fusion.67
  310.3 5.8 %all-to-all-done.3 = bf16[8,8,1536]{2,1,0:T(8,128)(2,1)S(1)} async-done(((bf16[8,8,1536]{2,1,0:T(8,128)(2,1)}), bf16[8,8,1536]{2,1,0:T(8,128)(2,1)S(1)}, u32[]{:S(2)}, u32[]{:S(2)}) %all-to-all-start.3) | async-done | bytes 196640 | tf_op jit(solution)/shard_map/all_to_all | solution.py:119
  316.2 0.2 reshape.289
  316.3 6.1 %fusion.85 = (f32[8,48]{1,0:T(8,128)S(1)}, f32[8,48,2048]{2,1,0:T(8,128)S(1)}) fusion(bf16[8,48,256]{2,1,0:T(8,128)(2,1)S(1)} %reshape.289, bf16[8,2048,256]{2,1,0:T(8,128)(2,1)} %param.14, pred[8,2048]{1,0:T(8,128)(4,1)S(1)} %iota_compare_fusion), kind=kOutput, calls=%fused_computation.121 | convolution fusion | flops 405012096 | bytes 11748864 | tf_op jit(solution)/shard_map/rhd,rsd->rhs/dot_general | solution.py:50
  322.4 0.2 fusion.86
  322.6 0.6 fusion.7
  323.2 0.3 fusion.49
  323.5 5.0 %fusion.30 = bf16[8,48,256]{2,1,0:T(8,128)(2,1)S(1)} fusion(f32[8,48,256]{2,1,0:T(8,128)S(1)} %fusion.49, bf16[8,2048,256]{2,1,0:T(8,128)(2,1)} %param.15, f32[8,48,2048]{2,1,0:T(8,128)S(1)} %get-tuple-element.34, f32[8,48]{1,0:T(8,128)S(1)} %max.13, f32[8,48]{1,0:T(8,128)S(1)} %add.105), kind=kOutput, calls=%fused_computation.26 | convolution fusion | flops 404520960 | bytes 12127232 | tf_op jit(solution)/shard_map/rhs,rsd->rhd/dot_general | solution.py:59
  328.4 0.2 all_to_all.92
  328.7 8.6 %all_to_all.103 = bf16[8,8,1536]{2,0,1:T(8,128)(2,1)S(1)} all-to-all(bf16[8,8,1536]{2,0,1:T(8,128)(2,1)S(1)} %copy.94), channel_id=1, replica_groups=mesh['gx'=4,'yz'=8] {'yz'}, dimensions={1} | all-to-all | bytes 393216 | tf_op jit(solution)/shard_map/all_to_all | solution.py:135
  337.3 18.1 %all_gather.11 = bf16[256,1536]{1,0:T(8,128)(2,1)S(1)} all-gather(bf16[64,1536]{1,0:T(8,128)(2,1)S(1)} %bitcast.57), channel_id=1, replica_groups=mesh['gx'=4,'yz'=8] {'gx'}, dimensions={0}, use_global_device_ids=true | all-gather | bytes 983040 | tf_op jit(solution)/shard_map/all_gather | solution.py:139
  355.4 10.5 %fusion.90 = f32[256,4608]{1,0:T(8,128)} fusion(bf16[256,1536]{1,0:T(8,128)(2,1)S(1)} %all_gather.11, bf16[1536,4608]{1,0:T(8,128)(2,1)} %param.13), kind=kOutput, calls=%fused_computation.126 | convolution fusion | flops 3623878656 | bytes 19660800 | tf_op jit(solution)/shard_map/dot_general | solution.py:138
  365.9 0.6 pad_maximum_fusion.5
  366.5 51.0 %reduce-scatter.11.cloned.1.call-done = f32[32,4608]{1,0:T(8,128)} async-done(((f32[256,4608]{1,0:T(8,128)}), f32[32,4608]{1,0:T(8,128)}) %reduce-scatter.11.cloned.1.call-update) | async-done | bytes 589840 | tf_op jit(solution)/shard_map/reduce_scatter | solution.py:143
  417.5 1.1 fusion.39
  418.6 0.9 pad_maximum_fusion.2
  (71 shorter events, 1.5 us)
Async XLA Ops:
  7.2 24.9 %copy-start = (bf16[4608,64]{0,1:T(8,128)(2,1)S(1)}, bf16[4608,64]{0,1:T(8,128)(2,1)}, u32[]{:S(2)}) copy-start(bf16[4608,64]{0,1:T(8,128)(2,1)} %param.12) | copy-start | bytes 1769476
  7.2 15.7 %copy-start.2 = (bf16[256,4608]{1,0:T(8,128)(2,1)S(1)}, bf16[256,4608]{1,0:T(8,128)(2,1)}, u32[]{:S(2)}) copy-start(bf16[256,4608]{1,0:T(8,128)(2,1)} %param.9) | copy-start | bytes 7077892
  7.2 24.9 %copy-start.3 = (f32[4608]{0:T(1024)S(1)}, f32[4608]{0:T(1024)}, u32[]{:S(2)}) copy-start(f32[4608]{0:T(1024)} %param.10) | copy-start | bytes 55300
  7.2 71.5 %reduce-scatter.5.cloned.1.call-start = ((), (), s32[]{:S(2)}) async-start(), calls=%async_computation.10 | async-start | bytes 2129920 | tf_op jit(solution)/shard_map/reduce_scatter | solution.py:105
  40.2 1.4 copy-start.8
  40.3 2.9 copy-start.9
  41.6 1.6 copy-start.5
  80.2 8.7 %all-to-all-start.1 = ((bf16[8,2,256]{2,1,0:T(2,128)(2,1)}), bf16[8,2,256]{2,1,0:T(2,128)(2,1)}, u32[]{:S(2)}, u32[]{:S(2)}) async-start(bf16[8,2,256]{2,1,0:T(2,128)(2,1)} %reshape.292), calls=%async_computation.2 | async-start | bytes 16384 | tf_op jit(solution)/shard_map/all_to_all | solution.py:120
  88.9 10.3 %all-to-all-start = ((bf16[8,8,1536]{2,1,0:T(8,128)(2,1)}), bf16[8,8,1536]{2,1,0:T(8,128)(2,1)S(1)}, u32[]{:S(2)}, u32[]{:S(2)}) async-start(bf16[8,8,1536]{2,1,0:T(8,128)(2,1)} %convert_element_type.94), calls=%async_computation.1 | async-start | bytes 393216 | tf_op jit(solution)/shard_map/all_to_all | solution.py:119
  93.0 104.5 %reduce-scatter.7.cloned.1.call-start = ((), (), s32[]{:S(2)}) async-start(), calls=%async_computation.11 | async-start | bytes 5308416 | tf_op jit(solution)/shard_map/reduce_scatter | solution.py:143
  99.5 7.0 %slice-start = ((s8[8388608]{0:T(1024)(128)(4,1)}), s8[4194304]{0:T(1024)(128)(4,1)S(1)}, s32[]{:S(2)}) async-start(s8[8388608]{0:T(1024)(128)(4,1)} %bitcast.51), calls=%async_computation.15 | async-start | bytes 8388608
  99.6 6.9 %slice-start.1 = ((s8[8388608]{0:T(1024)(128)(4,1)}), s8[4194304]{0:T(1024)(128)(4,1)S(1)}, s32[]{:S(2)}) async-start(s8[8388608]{0:T(1024)(128)(4,1)} %bitcast.51), calls=%async_computation.16 | async-start | bytes 8388608
  145.7 73.4 %copy-start.4 = (f32[4608]{0:T(1024)S(1)}, f32[4608]{0:T(1024)}, u32[]{:S(2)}) copy-start(f32[4608]{0:T(1024)} %param.10) | copy-start | bytes 55300
  145.7 102.0 %all-gather.2.cloned.1.call-start = ((), (), s32[]{:S(2)}) async-start(), calls=%async_computation.12 | async-start | bytes 2654208 | tf_op jit(solution)/shard_map/all_gather | solution.py:147
  219.9 76.8 %reduce-scatter.9.cloned.1.call-start = ((), (), s32[]{:S(2)}) async-start(), calls=%async_computation.13 | async-start | bytes 2129920 | tf_op jit(solution)/shard_map/reduce_scatter | solution.py:105
  259.2 51.0 %copy-start.6 = (f32[128]{0:T(128)S(1)}, f32[128]{0:T(128)}, u32[]{:S(2)}) copy-start(f32[128]{0:T(128)} %copy-done.5) | copy-start | bytes 1540
  259.2 51.0 %copy-start.7 = (f32[8]{0:T(128)S(1)}, f32[8]{0:T(128)}, u32[]{:S(2)}) copy-start(f32[8]{0:T(128)} %get-tuple-element.21) | copy-start | bytes 100
  298.2 8.4 %all-to-all-start.4 = ((bf16[8,2,256]{2,1,0:T(2,128)(2,1)}), bf16[8,2,256]{2,1,0:T(2,128)(2,1)S(1)}, u32[]{:S(2)}, u32[]{:S(2)}) async-start(bf16[8,2,256]{2,1,0:T(2,128)(2,1)} %reshape.294), calls=%async_computation.7 | async-start | bytes 16384 | tf_op jit(solution)/shard_map/all_to_all | solution.py:120
  306.5 9.6 %all-to-all-start.3 = ((bf16[8,8,1536]{2,1,0:T(8,128)(2,1)}), bf16[8,8,1536]{2,1,0:T(8,128)(2,1)S(1)}, u32[]{:S(2)}, u32[]{:S(2)}) async-start(bf16[8,8,1536]{2,1,0:T(8,128)(2,1)} %convert_element_type.104), calls=%async_computation.6 | async-start | bytes 393216 | tf_op jit(solution)/shard_map/all_to_all | solution.py:119
  309.9 107.5 %reduce-scatter.11.cloned.1.call-start = ((), (), s32[]{:S(2)}) async-start(), calls=%async_computation.14 | async-start | bytes 5308416 | tf_op jit(solution)/shard_map/reduce_scatter | solution.py:143
  365.9 53.6 %copy-start.1 = (bf16[4608,64]{0,1:T(8,128)(2,1)S(1)}, bf16[4608,64]{0,1:T(8,128)(2,1)}, u32[]{:S(2)}) copy-start(bf16[4608,64]{0,1:T(8,128)(2,1)} %param.12) | copy-start | bytes 1769476
Sparse Core Ops, SparseCore 0:
  41.7 36.9 reduce-scatter.4
  145.8 51.5 reduce-scatter.6
  220.1 27.6 all-gather.1
  259.4 37.3 reduce-scatter.8
  366.0 51.4 reduce-scatter.10
where the time goes:
time: 427 us; the launch traced here: 426 us
  waiting for transfers between devices  216 us (51%)
  blocking collectives  95.5 us (22%)
  matrix products  58.7 us (14%)
  starting transfers between devices  15.3 us (4%)
  other arithmetic  15.3 us (4%)
  between operations  14.2 us (3%)
  local copies, waits for them, and re-layouts  10.9 us (3%)
    reduce_scatter x2, waiting for transfers between devices, on_device(): lax.psum_scatter(partial_out, 'yz', scatter_dimension=0, tiled=True)  103 us
    reduce_scatter x2, waiting for transfers between devices, on_device(): lax.psum_scatter(project(jnp.int32(0), block_rows * lax.axis_size('gx')),...  72.9 us
    all_gather x2, blocking collectives, on_device(): lax.all_gather(heads_block, 'gx', axis=0, tiled=True)  36.3 us
    all_gather x1, waiting for transfers between devices, on_device(): lax.all_gather(layer_norm(own_rows, norm_gain), 'yz', axis=0, tiled=True)  27.8 us
    psum x2, blocking collectives, layer_norm(): totals = lax.psum(jnp.sum(values, axis=1), 'gx')  25.2 us
    dot_general x2, matrix products, on_device(): jnp.dot(lax.all_gather(heads_block, 'gx', axis=0, tiled=True), w_out, pre...  20.9 us
    all_to_all x2, blocking collectives, on_device(): lax.all_to_all(attended.reshape(row_dev, -1), 'yz', split_axis=1, concat_...  17.3 us
    psum x2, blocking collectives, layer_norm(): spread = lax.psum(jnp.sum(offset * offset, axis=1), 'gx') / D  16.7 us
  transfers between devices with their start and end apart: 9, of which 8 were waited for; matrix products, arithmetic and copies ran while one was open for 3% of the time, Pallas kernels for 0%

commit v1 on v0

v1 whole, which is shorter than its diff:
```python
import functools
import math

import jax
import jax.numpy as jnp
import numpy as np
from jax import lax
from jax.experimental import pallas as pl
from jax.experimental.pallas import tpu as pltpu
from jax.sharding import PartitionSpec as P

D = 18432
DH = 256
STEPS = 2
MESH = pl.DeviceIdType.MESH
VMEM_LIMIT = 48 * 1024 * 1024

epsilon = 1e-06
floor_score = -1e30
frequencies = np.exp(np.arange(DH // 2) * (-2.0 * math.log(10000.0) / DH)).astype(np.float32)


def params(collective_id):
    return pltpu.CompilerParams(
        collective_id=collective_id, has_side_effects=True, vmem_limit_bytes=VMEM_LIMIT
    )


def greet(targets):
    barrier = pltpu.get_barrier_semaphore()
    for target in targets:
        pl.semaphore_signal(barrier, inc=1, device_id=target, device_id_type=MESH)
    pl.semaphore_wait(barrier, len(targets))


def send(src, dst, send_sem, recv_sem, target):
    return pltpu.make_async_remote_copy(
        src_ref=src,
        dst_ref=dst,
        send_sem=send_sem,
        recv_sem=recv_sem,
        device_id=target,
        device_id_type=MESH,
    )


def turn(vectors, cosine, sine_part):
    leading = vectors[..., : DH // 2]
    trailing = vectors[..., DH // 2 :]
    return jnp.concatenate(
        [leading * cosine - trailing * sine_part, trailing * cosine + leading * sine_part], axis=-1
    )


def angles_of(places):
    angles = places.astype(jnp.float32)[..., None] * jnp.asarray(frequencies)
    return jnp.cos(angles), jnp.sin(angles)


def share_kernel(n, x_ref, out_ref, send_sem, recv_sem):
    me = lax.axis_index("gx")
    others = [lax.rem(me + k, n) for k in range(1, n)]
    greet([{"gx": other} for other in others])
    out_ref[me] = x_ref[...]
    copies = [
        send(x_ref, out_ref.at[me], send_sem.at[k], recv_sem.at[k], {"gx": other})
        for k, other in enumerate(others)
    ]
    for copy in copies:
        copy.start()
    for copy in copies:
        copy.wait()


def share(x, n):
    return pl.pallas_call(
        functools.partial(share_kernel, n),
        out_shape=jax.ShapeDtypeStruct((n,) + x.shape, x.dtype),
        in_specs=[pl.BlockSpec(memory_space=pltpu.VMEM)],
        out_specs=pl.BlockSpec(memory_space=pltpu.VMEM),
        scratch_shapes=[pltpu.SemaphoreType.DMA((n - 1,)), pltpu.SemaphoreType.DMA((n - 1,))],
        compiler_params=params(1),
    )(x)


def layer_norm(hidden, norm_gain, n):
    values = hidden.astype(jnp.float32)
    width = values.shape[1]
    mean_here = jnp.sum(values, axis=1) / width
    offset = values - mean_here[:, None]
    square_here = jnp.sum(offset * offset, axis=1)
    both = jnp.concatenate(
        [mean_here[None], square_here[None], jnp.zeros((6, values.shape[0]), jnp.float32)]
    )
    every = share(both, n)
    means, squares = every[:, 0], every[:, 1]
    center = jnp.sum(means, axis=0) / n
    shift = means - center[None]
    spread = (jnp.sum(squares, axis=0) + width * jnp.sum(shift * shift, axis=0)) / (width * n)
    return ((values - center[:, None]) * lax.rsqrt(spread + epsilon)[:, None] * norm_gain).astype(
        jnp.bfloat16
    )


def project_kernel(
    ng, ny, heads, rows, x_ref, wq_ref, wkv_ref, cos_ref, sin_ref, out_ref,
    own, pair_out, pair_in, far_in, kv_own, kv_pair_out, kv_pair_in, kv_far_in, stage, second, third,
    pair_send, pair_recv, far_send, far_recv,
    kv_pair_send, kv_pair_recv, kv_far_send, kv_far_recv, a2a_send_sem, a2a_recv_sem,
):
    step = pl.program_id(0)
    g = lax.axis_index("gx")
    y = lax.axis_index("yz")
    block = rows * ny
    half = ng // 2
    side = lax.rem(g, 2)
    group = g // 2
    partner = g + 1 - 2 * side
    groups = [lax.rem(group + k, half) for k in range(1, half)]
    y_others = [lax.rem(y + k, ny) for k in range(1, ny)]

    @pl.when(step == 0)
    def _():
        greet(
            [{"gx": partner}]
            + [{"gx": 2 * other + side} for other in groups]
            + [{"yz": other} for other in y_others]
        )

    def pair_copy(j):
        return send(pair_out.at[j], pair_in.at[j], pair_send.at[j], pair_recv.at[j], {"gx": partner})

    def far_copies(j):
        return [
            send(own.at[j, other], far_in.at[j, k], far_send.at[j, k], far_recv.at[j, k], {"gx": 2 * other + side})
            for k, other in enumerate(groups)
        ]

    def kv_pair_copy():
        return send(kv_pair_out, kv_pair_in, kv_pair_send, kv_pair_recv, {"gx": partner})

    def kv_far_copies():
        return [
            send(kv_own.at[other], kv_far_in.at[k], kv_far_send.at[k], kv_far_recv.at[k], {"gx": 2 * other + side})
            for k, other in enumerate(groups)
        ]

    def combine(j):
        pair_copy(j).wait()
        own[j] = own[j] + pair_in[j]
        for copy in far_copies(j):
            copy.start()

    product = jnp.dot(x_ref[...], wq_ref[...], preferred_element_type=jnp.float32)
    product = product.reshape(half, 2, block, DH)
    own[step] = jnp.where(side == 0, product[:, 0], product[:, 1])
    pair_out[step] = jnp.where(side == 0, product[:, 1], product[:, 0])
    pair_copy(step).start()

    @pl.when(step == 0)
    def _():
        small = jnp.dot(x_ref[...], wkv_ref[...], preferred_element_type=jnp.float32)
        small = jnp.concatenate(
            [small, jnp.zeros((small.shape[0], 128 - small.shape[1]), jnp.float32)], axis=1
        ).reshape(half, 2, block, 128)
        kv_own[...] = jnp.where(side == 0, small[:, 0], small[:, 1])
        kv_pair_out[...] = jnp.where(side == 0, small[:, 1], small[:, 0])
        kv_pair_copy().start()
        stage[...] = jnp.zeros_like(stage)

    @pl.when(step > 0)
    def _():
        combine(step - 1)

    @pl.when(step == heads - 1)
    def _():
        kv_pair_copy().wait()
        kv_own[...] = kv_own[...] + kv_pair_in[...]
        for copy in kv_far_copies():
            copy.start()
        combine(step)
        for j in range(heads):
            total = own[j, group]
            for k, copy in enumerate(far_copies(j)):
                copy.wait()
                total = total + far_in[j, k]
            turned = turn(total, cos_ref[...], sin_ref[...])
            stage[:, j * rows : (j + 1) * rows, :] = turned.reshape(ny, rows, DH)
        total = kv_own[group]
        for k, copy in enumerate(kv_far_copies()):
            copy.wait()
            total = total + kv_far_in[k]
        stage[:, heads * rows : (heads + 1) * rows, :128] = total.reshape(ny, rows, 128)
        second[...] = stage[...].astype(jnp.bfloat16)
        copies = [
            send(second.at[other], third.at[y], a2a_send_sem.at[k], a2a_recv_sem.at[k], {"yz": other})
            for k, other in enumerate(y_others)
        ]
        for copy in copies:
            copy.start()
        third[y] = second[y]
        for copy in copies:
            copy.wait()
        out_ref[...] = third[...]


def project(normed, w_query, w_keyval, cosine, sine_part, ng, ny, rows):
    total_rows, depth = normed.shape
    heads = w_query.shape[1] // DH
    narrow = w_keyval.shape[1]
    slots = (heads + 2) // 2 * 2
    block = rows * ny
    half = ng // 2
    dma = pltpu.SemaphoreType.DMA
    whole = lambda j: (0, 0)
    return pl.pallas_call(
        functools.partial(project_kernel, ng, ny, heads, rows),
        grid=(heads,),
        out_shape=jax.ShapeDtypeStruct((ny, slots * rows, DH), jnp.bfloat16),
        in_specs=[
            pl.BlockSpec((total_rows, depth), whole),
            pl.BlockSpec((depth, DH), lambda j: (0, j)),
            pl.BlockSpec((depth, narrow), whole),
            pl.BlockSpec((block, DH // 2), whole),
            pl.BlockSpec((block, DH // 2), whole),
        ],
        out_specs=pl.BlockSpec(memory_space=pltpu.VMEM),
        scratch_shapes=[
            pltpu.VMEM((heads, half, block, DH), jnp.float32),
            pltpu.VMEM((heads, half, block, DH), jnp.float32),
            pltpu.VMEM((heads, half, block, DH), jnp.float32),
            pltpu.VMEM((heads, half - 1, block, DH), jnp.float32),
            pltpu.VMEM((half, block, 128), jnp.float32),
            pltpu.VMEM((half, block, 128), jnp.float32),
            pltpu.VMEM((half, block, 128), jnp.float32),
            pltpu.VMEM((half - 1, block, 128), jnp.float32),
            pltpu.VMEM((ny, slots * rows, DH), jnp.float32),
            pltpu.VMEM((ny, slots * rows, DH), jnp.bfloat16),
            pltpu.VMEM((ny, slots * rows, DH), jnp.bfloat16),
            dma((heads,)),
            dma((heads,)),
            dma((heads, half - 1)),
            dma((heads, half - 1)),
            dma,
            dma,
            dma((half - 1,)),
            dma((half - 1,)),
            dma((ny - 1,)),
            dma((ny - 1,)),
        ],
        compiler_params=params(2),
    )(normed, w_query, w_keyval, cosine, sine_part)


def spread_kernel(ng, ny, x_ref, out_ref, send_sem, recv_sem):
    g = lax.axis_index("gx")
    y = lax.axis_index("yz")
    pairs = [(a, b) for a in range(ng) for b in range(ny) if a or b]
    places = [(lax.rem(g + a, ng), lax.rem(y + b, ny)) for a, b in pairs]
    greet([{"gx": to_g, "yz": to_y} for to_g, to_y in places])
    copies = [
        send(x_ref.at[to_y], out_ref.at[g, y], send_sem.at[k], recv_sem.at[k], {"gx": to_g, "yz": to_y})
        for k, (to_g, to_y) in enumerate(places)
    ]
    for copy in copies:
        copy.start()
    out_ref[g, y] = x_ref[y]
    for copy in copies:
        copy.wait()


def spread_heads(x, ng, ny):
    count = ng * ny - 1
    return pl.pallas_call(
        functools.partial(spread_kernel, ng, ny),
        out_shape=jax.ShapeDtypeStruct((ng,) + x.shape, x.dtype),
        in_specs=[pl.BlockSpec(memory_space=pltpu.VMEM)],
        out_specs=pl.BlockSpec(memory_space=pltpu.VMEM),
        scratch_shapes=[pltpu.SemaphoreType.DMA((count,)), pltpu.SemaphoreType.DMA((count,))],
        compiler_params=params(3),
    )(x)


def output_kernel(
    n, chunks, width, x_ref, w_ref, h_ref, out_ref,
    own, pair_out, pair_in, far_in, pair_send, pair_recv, far_send, far_recv,
):
    step = pl.program_id(0)
    me = lax.axis_index("yz")
    half = n // 2
    side = lax.rem(me, 2)
    group = me // 2
    partner = me + 1 - 2 * side
    groups = [lax.rem(group + k, half) for k in range(1, half)]
    rows = h_ref.shape[0]

    @pl.when(step == 0)
    def _():
        greet([{"yz": partner}] + [{"yz": 2 * other + side} for other in groups])

    def pair_copy(s):
        return send(pair_out.at[s], pair_in.at[s], pair_send.at[s], pair_recv.at[s], {"yz": partner})

    def far_copies(s):
        return [
            send(own.at[s, other], far_in.at[s, k], far_send.at[s, k], far_recv.at[s, k], {"yz": 2 * other + side})
            for k, other in enumerate(groups)
        ]

    def combine(s):
        pair_copy(s).wait()
        own[s] = own[s] + pair_in[s]
        for copy in far_copies(s):
            copy.start()

    product = jnp.dot(x_ref[...], w_ref[...], preferred_element_type=jnp.float32)
    product = product.reshape(half, 2, rows, width)
    own[step] = jnp.where(side == 0, product[:, 0], product[:, 1])
    pair_out[step] = jnp.where(side == 0, product[:, 1], product[:, 0])
    pair_copy(step).start()

    @pl.when(step > 0)
    def _():
        combine(step - 1)

    @pl.when(step == chunks - 1)
    def _():
        combine(step)
        for s in range(chunks):
            total = own[s, group]
            for k, copy in enumerate(far_copies(s)):
                copy.wait()
                total = total + far_in[s, k]
            columns = slice(s * width, (s + 1) * width)
            out_ref[:, columns] = (h_ref[:, columns].astype(jnp.float32) + total).astype(jnp.bfloat16)


def output(x, w_out, own_rows, n):
    total_rows, depth = x.shape
    rows, columns = own_rows.shape
    width = 768
    chunks = columns // width
    half = n // 2
    dma = pltpu.SemaphoreType.DMA
    return pl.pallas_call(
        functools.partial(output_kernel, n, chunks, width),
        grid=(chunks,),
        out_shape=jax.ShapeDtypeStruct((rows, columns), jnp.bfloat16),
        in_specs=[
            pl.BlockSpec((total_rows, depth), lambda j: (0, 0)),
            pl.BlockSpec((depth, width), lambda j: (0, j)),
            pl.BlockSpec((rows, columns), lambda j: (0, 0)),
        ],
        out_specs=pl.BlockSpec(memory_space=pltpu.VMEM),
        scratch_shapes=[
            pltpu.VMEM((chunks, half, rows, width), jnp.float32),
            pltpu.VMEM((chunks, half, rows, width), jnp.float32),
            pltpu.VMEM((chunks, half, rows, width), jnp.float32),
            pltpu.VMEM((chunks, half - 1, rows, width), jnp.float32),
            dma((chunks,)),
            dma((chunks,)),
            dma((chunks, half - 1)),
            dma((chunks, half - 1)),
        ],
        compiler_params=params(4),
    )(x, w_out, own_rows)


def gather_kernel(n, x_ref, out_ref, send_sem, recv_sem, pair_send, pair_recv):
    me = lax.axis_index("yz")
    half = n // 2
    side = lax.rem(me, 2)
    group = me // 2
    partner = me + 1 - 2 * side
    groups = [lax.rem(group + k, half) for k in range(1, half)]
    greet([{"yz": partner}] + [{"yz": 2 * other + side} for other in groups])
    copies = [
        send(x_ref, out_ref.at[me], send_sem.at[k], recv_sem.at[k], {"yz": 2 * other + side})
        for k, other in enumerate(groups)
    ]
    for copy in copies:
        copy.start()
    passed = [send(x_ref, out_ref.at[me], pair_send.at[half - 1], pair_recv.at[half - 1], {"yz": partner})]
    passed[0].start()
    out_ref[me] = x_ref[...]
    for k, copy in enumerate(copies):
        copy.wait_recv()
        source = 2 * lax.rem(group + half - 1 - k, half) + side
        passed.append(
            send(out_ref.at[source], out_ref.at[source], pair_send.at[k], pair_recv.at[k], {"yz": partner})
        )
        passed[-1].start()
    for copy in copies:
        copy.wait_send()
    for copy in passed:
        copy.wait()


def gather(x, n):
    half = n // 2
    dma = pltpu.SemaphoreType.DMA
    return pl.pallas_call(
        functools.partial(gather_kernel, n),
        out_shape=jax.ShapeDtypeStruct((n,) + x.shape, x.dtype),
        in_specs=[pl.BlockSpec(memory_space=pltpu.VMEM)],
        out_specs=pl.BlockSpec(memory_space=pltpu.VMEM),
        scratch_shapes=[dma((half - 1,)), dma((half - 1,)), dma((half,)), dma((half,))],
        compiler_params=params(5),
    )(x)


def attend(queries, key_cache, value_cache, lengths, extra_keys, extra_values):
    score_scale = 1.0 / math.sqrt(queries.shape[-1])
    extra_scores = (
        jnp.einsum("rhd,rtd->rht", queries, extra_keys, preferred_element_type=jnp.float32)
        * score_scale
    )
    scores = (
        jnp.einsum("rhd,rsd->rhs", queries, key_cache, preferred_element_type=jnp.float32)
        * score_scale
    )
    usable = jnp.arange(key_cache.shape[1])[None, :] < lengths[:, None]
    scores = jnp.where(usable[:, None, :], scores, floor_score)
    row_top = jnp.maximum(jnp.max(scores, axis=2), jnp.max(extra_scores, axis=2))[..., None]
    cached_weights = jnp.exp(scores - row_top)
    extra_weights = jnp.exp(extra_scores - row_top)
    weight_sum = jnp.sum(cached_weights, axis=2) + jnp.sum(extra_weights, axis=2)
    weighted = jnp.einsum(
        "rhs,rsd->rhd",
        cached_weights.astype(jnp.bfloat16),
        value_cache,
        preferred_element_type=jnp.float32,
    )
    weighted = weighted + jnp.einsum(
        "rht,rtd->rhd",
        extra_weights.astype(jnp.bfloat16),
        extra_values,
        preferred_element_type=jnp.float32,
    )
    return (weighted / weight_sum[..., None]).astype(jnp.bfloat16)


def on_device(
    states_in, norm_gain, w_query, w_keyval, w_out, key_cache, value_cache, lengths, positions
):
    ng = lax.axis_size("gx")
    ny = lax.axis_size("yz")
    g = lax.axis_index("gx")
    y = lax.axis_index("yz")
    rows = key_cache.shape[0]
    total_rows, features = states_in.shape
    block = total_rows // ng
    share_rows = total_rows // ny
    heads = w_query.shape[1] // DH
    own_positions = lax.dynamic_slice_in_dim(positions, (g * ny + y) * rows, rows)
    block_positions = lax.dynamic_slice_in_dim(positions, g * block, block)
    own_rows = lax.dynamic_slice_in_dim(states_in, y * share_rows, share_rows, 0)
    hidden = states_in
    new_keys = []
    new_values = []
    results = []
    for t in range(STEPS):
        normed = layer_norm(hidden, norm_gain, ng)
        cosine, sine_part = angles_of(block_positions + t)
        arrived = project(normed, w_query, w_keyval, cosine, sine_part, ng, ny, rows)
        arrived = arrived.reshape(ny, -1, rows, DH)
        queries = arrived[:, :heads].transpose(2, 0, 1, 3).reshape(rows, ny * heads, DH)
        keyval = arrived[:, heads, :, : w_keyval.shape[1]].transpose(1, 0, 2).reshape(rows, 2 * DH)
        key_new = turn(keyval[:, :DH].astype(jnp.float32), *angles_of(own_positions + t)).astype(
            jnp.bfloat16
        )
        new_keys.append(key_new)
        new_values.append(keyval[:, DH:])
        attended = attend(
            queries,
            key_cache,
            value_cache,
            lengths,
            jnp.stack(new_keys, axis=1),
            jnp.stack(new_values, axis=1),
        )
        parcels = attended.reshape(rows, ny, 2, heads * DH // 2).transpose(1, 0, 2, 3)
        spread = spread_heads(parcels.reshape(ny, 2 * rows, heads * DH // 2), ng, ny)
        own_rows = output(spread.reshape(total_rows, heads * DH), w_out, own_rows, ny)
        results.append(own_rows)
        if t + 1 < STEPS:
            hidden = gather(own_rows, ny).reshape(total_rows, features)
    new_kv = jnp.stack(
        [
            jnp.concatenate([key_part, value_part], axis=1)
            for key_part, value_part in zip(new_keys, new_values)
        ]
    )
    return (jnp.stack(results), new_kv)


def solution(mesh):
    in_specs = (
        P(None, "gx"),
        P("gx"),
        P("gx", "yz"),
        P("gx", "yz"),
        P("yz", "gx"),
        P(("gx", "yz"), None, None),
        P(("gx", "yz"), None, None),
        P(("gx", "yz")),
        P(),
    )
    out_specs = (P(None, "yz", "gx"), P(None, ("gx", "yz"), None))
    return jax.shard_map(
        on_device, mesh=mesh, in_specs=in_specs, out_specs=out_specs, check_vma=False
    )
```

time: 427 us -> 269 us (0.63)
  Pallas kernels: 0 us -> 221 us
  waiting for transfers between devices: 216 us -> 0 us
  blocking collectives: 95.5 us -> 0 us
  matrix products: 58.7 us -> 16.3 us
  starting transfers between devices: 15.3 us -> 0 us
  between operations: 14.2 us -> 1.27 us
    pallas_call x0 -> x9, Pallas kernels: none -> 221 us  [the longest x2 81.9 us: project(): pl.pallas_call(functools.partial(project_kernel, ng, ny, heads, rows), gr...]
    reduce_scatter x4 -> x0, waiting for transfers between devices: 176 us -> none  [the longest x2 103 us: on_device(): lax.psum_scatter(partial_out, 'yz', scatter_dimension=0, tiled=True)]
    psum x4 -> x0, blocking collectives: 41.9 us -> none  [the longest x2 25.2 us: layer_norm(): totals = lax.psum(jnp.sum(values, axis=1), 'gx')]
    dot_general x6 -> x0, matrix products: 39.2 us -> none  [the longest x2 20.9 us: on_device(): jnp.dot(lax.all_gather(heads_block, 'gx', axis=0, tiled=True), w_out, pre...]
    all_gather x2 -> x0, blocking collectives: 36.3 us -> none  [on_device(): lax.all_gather(heads_block, 'gx', axis=0, tiled=True)]
    all_gather x1 -> x0, waiting for transfers between devices: 27.8 us -> none  [on_device(): lax.all_gather(layer_norm(own_rows, norm_gain), 'yz', axis=0, tiled=True)]
    all_to_all x2 -> x0, blocking collectives: 17.3 us -> none  [on_device(): lax.all_to_all(attended.reshape(row_dev, -1), 'yz', split_axis=1, concat_...]
    all_to_all x4 -> x0, starting transfers between devices: 15.1 us -> none  [the longest x2 7.6 us: on_device(): lax.all_to_all(keyval_block, 'yz', split_axis=0, concat_axis=1, tiled=True)]
  transfers between devices with their start and end apart: 9 -> 0, of which waited for: 8 -> 0; matrix products, arithmetic and copies ran while one was open for 3% -> 0% of each run, Pallas kernels for 0% -> 0%
where the time goes in v1:
time: 269 us; the launch traced here: 267 us
  Pallas kernels  221 us (82%)
  matrix products  16.3 us (6%)
  other arithmetic  16.2 us (6%)
  local copies, waits for them, and re-layouts  12.1 us (4%)
    pallas_call x2, Pallas kernels, project(): pl.pallas_call(functools.partial(project_kernel, ng, ny, heads, rows), gr...  81.9 us
    pallas_call x2, Pallas kernels, output(): pl.pallas_call(functools.partial(output_kernel, n, chunks, width), grid=(...  68 us
    pallas_call x2, Pallas kernels, spread_heads(): pl.pallas_call(functools.partial(spread_kernel, ng, ny), out_shape=jax.Sh...  37.7 us
    pallas_call x1, Pallas kernels, gather(): pl.pallas_call(functools.partial(gather_kernel, n), out_shape=jax.ShapeDt...  17.7 us
    pallas_call x2, Pallas kernels, share(): pl.pallas_call(functools.partial(share_kernel, n), out_shape=jax.ShapeDty...  16 us
    dot_general x2, matrix products, attend(): jnp.einsum('rhd,rsd->rhs', queries, key_cache, preferred_element_type=jnp...  12.5 us
    unnamed x53, local copies, waits for them, and re-layouts  5.96 us

profile of v1, /device:TPU:0, one launch (start us, length us, event | category | flops | bytes accessed | tf_op | source)
XLA Modules:
  0.0 267.1 jit_solution(12752859056518349927)
XLA Ops:
  0.7 0.0 copy-start.9
  0.7 0.9 add_convert_fusion.1
  1.6 2.1 multiply_sine_fusion
  3.6 2.1 convert_reduce_fusion
  5.7 0.8 fusion.1
  6.5 0.1 pad.23.clone
  6.6 0.5 copy-done.20
  7.1 0.1 maximum_maximum_fusion.x_ref
  7.2 7.4 %shard_map.113 = f32[4,8,256]{2,1,0:T(8,128)S(1)} custom-call(f32[8,256]{1,0:T(8,128)S(1)} %maximum_maximum_fusion.x_ref), custom_call_target="tpu_custom_call" | custom-call | tf_op jit(solution)/shard_map/pallas_call | solution.py:76
  14.7 1.0 fusion.4.x_ref
  15.7 1.8 copy.102.wkv_ref
  17.5 0.0 copy-start.5
  17.5 0.7 copy-done.5
  18.3 0.8 copy-done.6
  19.0 41.0 %shard_map.114 = bf16[8,64,256]{2,1,0:T(8,128)(2,1)S(1)} custom-call(bf16[256,4608]{1,0:T(8,128)(2,1)S(1)} %fusion.4.x_ref, bf16[4608,1536]{1,0:T(8,128)(2,1)} %wq_ref.3, bf16[4608,64]{1,0:T(8,128)(2,1)S(1)} %copy.102.wkv_ref, f32[64,128]{1,0:T(8,128)S(1)} %copy-done.5, f32[64,128]{1,0:T(8,128)S(1)} %copy-done.6), custom_call_target="tpu_custom_call" | custom-call | tf_op jit(solution)/shard_map/pallas_call | solution.py:216
  60.0 0.7 copy-done.2
  60.7 0.1 reshape.231
  60.8 0.6 fusion.80
  61.4 0.6 add_convert_fusion
  62.0 0.1 fusion.69
  62.2 0.9 slice.64
  63.1 0.0 slice-start
  63.1 0.2 fusion.38
  63.3 0.9 iota_compare_fusion
  64.2 0.0 slice-start.1
  64.2 6.3 %fusion.82 = (f32[8,48]{1,0:T(8,128)S(1)}, f32[8,48,2048]{2,1,0:T(8,128)S(1)}) fusion(bf16[8,2048,256]{2,1,0:T(8,128)(2,1)} %param.15, bf16[8,48,256]{2,0,1:T(8,128)(2,1)S(1)} %bitcast.85, pred[8,2048]{1,0:T(8,128)(4,1)S(1)} %iota_compare_fusion), kind=kOutput, calls=%fused_computation.124 | convolution fusion | flops 405012096 | bytes 11748864 | tf_op jit(solution)/shard_map/rhd,rsd->rhs/dot_general | solution.py:419
  70.5 0.6 fusion.8
  71.1 1.6 fusion.30
  72.7 0.1 reshape.232
  72.9 0.1 copy.142
  73.0 0.1 reshape.233.x_ref
  73.1 19.1 %shard_map.115 = bf16[4,8,16,768]{3,2,1,0:T(8,128)(2,1)S(1)} custom-call(bf16[8,16,768]{2,1,0:T(8,128)(2,1)S(1)} %reshape.233.x_ref), custom_call_target="tpu_custom_call" | custom-call | tf_op jit(solution)/shard_map/pallas_call | solution.py:274
  92.2 0.3 reshape.234.x_ref
  92.4 1.0 constant_dynamic-slice_fusion.h_ref
  93.4 34.0 %shard_map.116.x_ref.h_ref = bf16[32,4608]{1,0:T(8,128)(2,1)S(1)} custom-call(bf16[256,1536]{1,0:T(8,128)(2,1)S(1)} %reshape.234.x_ref, bf16[1536,4608]{1,0:T(8,128)(2,1)} %w_ref.3, bf16[32,4608]{1,0:T(8,128)(2,1)S(1)} %constant_dynamic-slice_fusion.h_ref), custom_call_target="tpu_custom_call" | custom-call | tf_op jit(solution)/shard_map/pallas_call | solution.py:345
  127.4 17.7 %shard_map.117 = bf16[8,32,4608]{2,1,0:T(8,128)(2,1)S(1)} custom-call(bf16[32,4608]{1,0:T(8,128)(2,1)S(1)} %shard_map.116.x_ref.h_ref), custom_call_target="tpu_custom_call" | custom-call | tf_op jit(solution)/shard_map/pallas_call | solution.py:402
  145.1 0.0 copy-start
  145.1 0.7 copy-done
  145.8 0.4 convert_reduce_fusion.1
  146.2 0.6 copy-done.10
  146.8 1.4 multiply_reduce_fusion
  148.2 1.3 broadcast_in_dim.23
  149.5 1.3 div.45
  150.9 0.7 maximum_maximum_fusion.1.x_ref
  151.6 8.6 %shard_map.118 = f32[4,8,256]{2,1,0:T(8,128)S(1)} custom-call(f32[8,256]{1,0:T(8,128)S(1)} %maximum_maximum_fusion.1.x_ref), custom_call_target="tpu_custom_call" | custom-call | tf_op jit(solution)/shard_map/pallas_call | solution.py:76
  160.3 1.7 fusion.7.x_ref
  162.0 0.0 copy-start.18
  162.1 40.9 %shard_map.119 = bf16[8,64,256]{2,1,0:T(8,128)(2,1)S(1)} custom-call(bf16[256,4608]{1,0:T(8,128)(2,1)S(1)} %fusion.7.x_ref, bf16[4608,1536]{1,0:T(8,128)(2,1)} %wq_ref.3, bf16[4608,64]{1,0:T(8,128)(2,1)S(1)} %copy.102.wkv_ref, f32[64,128]{1,0:T(8,128)S(1)} %copy-done.4, f32[64,128]{1,0:T(8,128)S(1)} %copy-done.3), custom_call_target="tpu_custom_call" | custom-call | tf_op jit(solution)/shard_map/pallas_call | solution.py:216
  203.0 0.1 reshape.237
  203.1 0.1 fusion.65
  203.3 0.6 pad_maximum_fusion.1
  203.9 0.0 slice-start.2
  203.9 6.2 %fusion.83 = (f32[8,48]{1,0:T(8,128)S(1)}, f32[8,48,2048]{2,1,0:T(8,128)S(1)}) fusion(bf16[8,2048,256]{2,1,0:T(8,128)(2,1)} %param.15, bf16[8,48,256]{2,0,1:T(8,128)(2,1)S(1)} %bitcast.82, pred[8,2048]{1,0:T(8,128)(4,1)S(1)} %iota_compare_fusion), kind=kOutput, calls=%fused_computation.125 | convolution fusion | flops 405012096 | bytes 11748864 | tf_op jit(solution)/shard_map/rhd,rsd->rhs/dot_general | solution.py:419
  210.2 0.2 fusion.84
  210.4 0.6 fusion.10
  211.1 0.3 fusion.48
  211.3 1.6 fusion.33
  212.9 0.1 reshape.238
  213.1 0.1 copy.141
  213.2 0.1 reshape.239.x_ref
  213.3 18.6 %shard_map.120 = bf16[4,8,16,768]{3,2,1,0:T(8,128)(2,1)S(1)} custom-call(bf16[8,16,768]{2,1,0:T(8,128)(2,1)S(1)} %reshape.239.x_ref), custom_call_target="tpu_custom_call" | custom-call | tf_op jit(solution)/shard_map/pallas_call | solution.py:274
  231.9 0.3 reshape.240.x_ref
  232.2 34.0 %shard_map.121 = bf16[32,4608]{1,0:T(8,128)(2,1)S(1)} custom-call(bf16[256,1536]{1,0:T(8,128)(2,1)S(1)} %reshape.240.x_ref, bf16[1536,4608]{1,0:T(8,128)(2,1)} %w_ref.3, bf16[32,4608]{1,0:T(8,128)(2,1)S(1)} %copy-done.1), custom_call_target="tpu_custom_call" | custom-call | tf_op jit(solution)/shard_map/pallas_call | solution.py:345
  266.2 0.9 pad_maximum_fusion
  (71 shorter events, 0.4 us)
Async XLA Ops:
  0.6 5.1 %copy-start.7 = (bf16[256,4608]{1,0:T(8,128)(2,1)S(1)}, bf16[256,4608]{1,0:T(8,128)(2,1)}, u32[]{:S(2)}) copy-start(bf16[256,4608]{1,0:T(8,128)(2,1)} %param.10) | copy-start | bytes 7077892
  0.6 14.0 %copy-start.8 = (bf16[256,4608]{1,0:T(8,128)(2,1)S(1)}, bf16[256,4608]{1,0:T(8,128)(2,1)}, u32[]{:S(2)}) copy-start(bf16[256,4608]{1,0:T(8,128)(2,1)} %param.10) | copy-start | bytes 7077892
  0.7 14.0 %copy-start.9 = (f32[4608]{0:T(1024)S(1)}, f32[4608]{0:T(1024)}, u32[]{:S(2)}) copy-start(f32[4608]{0:T(1024)} %param.11) | copy-start | bytes 55300
  6.6 0.5 copy-start.20
  17.5 0.8 copy-start.5
  18.3 0.8 copy-start.6
  19.0 42.4 %copy-start.21 = (s32[256]{0:T(256)S(1)}, s32[256]{0:T(256)}, u32[]{:S(2)}) copy-start(s32[256]{0:T(256)} %param.18) | copy-start | bytes 3076
  19.0 43.0 %copy-start.17 = (f32[128]{0:T(128)S(1)}, f32[128]{0:T(128)}, u32[]{:S(2)}) copy-start(f32[128]{0:T(128)} %constant.49.clone) | copy-start | bytes 1540
  60.0 0.7 copy-start.2
  62.2 1.2 copy-start.11
  62.2 8.3 %copy-start.13 = (bf16[8,128]{1,0:T(8,128)(2,1)}, bf16[8,128]{1,0:T(8,128)(2,1)S(1)}, u32[]{:S(2)}) copy-start(bf16[8,128]{1,0:T(8,128)(2,1)S(1)} %get-tuple-element.10) | copy-start | bytes 6148
  63.1 8.0 %slice-start = ((s8[8388608]{0:T(1024)(128)(4,1)}), s8[4194304]{0:T(1024)(128)(4,1)S(1)}, s32[]{:S(2)}) async-start(s8[8388608]{0:T(1024)(128)(4,1)} %bitcast.76), calls=%async_computation | async-start | bytes 8388608
  64.2 6.9 %slice-start.1 = ((s8[8388608]{0:T(1024)(128)(4,1)}), s8[4194304]{0:T(1024)(128)(4,1)S(1)}, s32[]{:S(2)}) async-start(s8[8388608]{0:T(1024)(128)(4,1)} %bitcast.76), calls=%async_computation.1 | async-start | bytes 8388608
  145.1 0.7 copy-start
  146.2 0.6 copy-start.10
  150.8 11.2 %copy-start.3 = (f32[64,128]{1,0:T(8,128)S(1)}, f32[64,128]{1,0:T(8,128)}, u32[]{:S(2)}) copy-start(f32[64,128]{1,0:T(8,128)} %get-tuple-element.23.sin_ref) | copy-start | bytes 98308
  150.9 11.2 %copy-start.4 = (f32[64,128]{1,0:T(8,128)S(1)}, f32[64,128]{1,0:T(8,128)}, u32[]{:S(2)}) copy-start(f32[64,128]{1,0:T(8,128)} %get-tuple-element.24.cos_ref) | copy-start | bytes 98308
  162.0 41.1 %copy-start.18 = (f32[128]{0:T(128)S(1)}, f32[128]{0:T(128)}, u32[]{:S(2)}) copy-start(f32[128]{0:T(128)} %constant.49.clone) | copy-start | bytes 1540
  162.0 41.1 %copy-start.19 = (f32[8]{0:T(128)S(1)}, f32[8]{0:T(128)}, u32[]{:S(2)}) copy-start(f32[8]{0:T(128)} %get-tuple-element.21) | copy-start | bytes 100
  162.1 41.2 %copy-start.12 = (bf16[8,128]{1,0:T(8,128)(2,1)S(1)}, bf16[8,128]{1,0:T(8,128)(2,1)}, u32[]{:S(2)}) copy-start(bf16[8,128]{1,0:T(8,128)(2,1)} %copy-done.11) | copy-start | bytes 6148
  162.1 41.2 %copy-start.14 = (bf16[8,128]{1,0:T(8,128)(2,1)S(1)}, bf16[8,128]{1,0:T(8,128)(2,1)}, u32[]{:S(2)}) copy-start(bf16[8,128]{1,0:T(8,128)(2,1)} %copy-done.13) | copy-start | bytes 6148
  162.1 41.2 %copy-start.16 = (bf16[8,256]{1,0:T(8,128)(2,1)S(1)}, bf16[8,256]{1,0:T(8,128)(2,1)}, u32[]{:S(2)}) copy-start(bf16[8,256]{1,0:T(8,128)(2,1)} %get-tuple-element.12) | copy-start | bytes 12292
  203.9 7.4 %slice-start.2 = ((s8[8388608]{0:T(1024)(128)(4,1)}), s8[4194304]{0:T(1024)(128)(4,1)S(1)}, s32[]{:S(2)}) async-start(s8[8388608]{0:T(1024)(128)(4,1)} %bitcast.78), calls=%async_computation.2 | async-start | bytes 8388608
  203.9 7.4 %slice-start.3 = ((s8[8388608]{0:T(1024)(128)(4,1)}), s8[4194304]{0:T(1024)(128)(4,1)S(1)}, s32[]{:S(2)}) async-start(s8[8388608]{0:T(1024)(128)(4,1)} %bitcast.78), calls=%async_computation.3 | async-start | bytes 8388608
  210.2 0.9 copy-start.15
  212.9 19.3 %copy-start.1 = (bf16[32,4608]{1,0:T(8,128)(2,1)S(1)}, bf16[32,4608]{1,0:T(8,128)(2,1)}, u32[]{:S(2)}) copy-start(bf16[32,4608]{1,0:T(8,128)(2,1)} %copy-done) | copy-start | bytes 884740
